TPU v7x, 512 devices: a whole 4x4x16 slice. The times are simulated.
512 devices in a mesh: tok: 16 (over z), vocab: 16 (over y, x_lo, core), grp: 2 (over x_hi).
Axes of the slice: x: 4 (x_hi: 2, x_lo: 2; x = x_hi * 2 + x_lo), y: 4, z: 16, core: 2. Of those that a mesh axis runs over, the one named last changes fastest.
Arguments:
- logits: bfloat16 [2, 2048, 131072], P('grp', 'tok', 'vocab'), may hold values from -60 to 440
- segment_ids: int32 [2048], P('tok'), may hold values from 0 to 7, as said below
- token_mask: int32 [2048], P('tok'), may hold values from 0 to 1, as said below
- student_head: bfloat16 [32, 16, 256, 1792], P(('vocab', 'grp'), 'tok'), may hold values from -6 to 6
Outputs:
- gradient: bfloat16 [2048, 131072], P('tok', ('vocab', 'grp'))
- hidden_grad: float32 [2048, 1792], P('tok', 'grp')
- distill_loss_total: float32 [], replicated
Inputs may be any that keep to these rules, and one draw needn't show every extreme that they name: `segment_ids`: ids never fall along the tokens, and each of the 8 documents holds at least one token. `token_mask`: every document holds at least one token with mask 1.
All inputs are finite; a program needn't handle non-finite values.
Results may differ from a plain program's by a relative error of at most 0.0034.
Values may be sent and summed in bfloat16 or wider, within the bound.
A program may use at most 64 MiB of HBM per device.

v0:
```python
import jax
import jax.numpy as jnp
from jax import lax
from jax.sharding import PartitionSpec as P

SEGS = 8


SOFTEN_FACTOR = 2.0


def swapped(value, axis, apart):
    mask = 2**apart
    pairs = [(source, source ^ mask) for source in range(lax.axis_size(axis))]
    return lax.ppermute(value, axis, pairs)


def divergence(teacher_tempered, student_tempered, teacher_lse, student_lse, token_factor):
    log_teacher = teacher_tempered - teacher_lse[:, None]
    log_student = student_tempered - student_lse[:, None]
    teacher_probs = jnp.exp(log_teacher)
    student_probs = jnp.exp(log_student)
    kl_part = jnp.sum(teacher_probs * (log_teacher - log_student), axis=1)
    gradient_slice = (
        SOFTEN_FACTOR * token_factor[:, None] * (student_probs - teacher_probs)
    ).astype(jnp.bfloat16)
    return (gradient_slice, kl_part)


def per_device(logits, segment_ids, token_mask, student_head):
    resident_tile = logits[0]
    tok_rows = resident_tile.shape[0]
    half_columns = resident_tile.shape[1] // 2
    group_index = lax.axis_index("grp")
    token_total_count = tok_rows * lax.axis_size("tok")
    doc_len = token_total_count // SEGS
    doc_labels = jnp.arange(SEGS, dtype=jnp.int32)
    membership = (segment_ids[:, None] == doc_labels[None, :]).astype(jnp.float32)
    masked = token_mask.astype(jnp.float32)
    local_counts = jnp.sum(membership * masked[:, None], axis=0)
    doc_sizes = lax.psum(local_counts, "tok")
    own_size = jnp.sum(membership * doc_sizes[None, :], axis=1)
    token_factor = masked * doc_len / own_size
    tempered_logits = resident_tile.astype(jnp.float32) / SOFTEN_FACTOR
    row_top = lax.pmax(jnp.max(tempered_logits, axis=1), "vocab")
    row_mass = lax.psum(jnp.sum(jnp.exp(tempered_logits - row_top[:, None]), axis=1), "vocab")
    own_lse = row_top + jnp.log(row_mass)
    other_top, other_mass = swapped((row_top, row_mass), "grp", 0)
    other_lse = other_top + jnp.log(other_mass)
    teacher_lse = jnp.where(group_index == 0, own_lse, other_lse)
    student_lse = jnp.where(group_index == 0, other_lse, own_lse)
    exchanged_half = lax.all_to_all(resident_tile, "grp", split_axis=1, concat_axis=1, tiled=True)
    teacher_tempered = exchanged_half[:, :half_columns].astype(jnp.float32) / SOFTEN_FACTOR
    student_tempered = exchanged_half[:, half_columns:].astype(jnp.float32) / SOFTEN_FACTOR
    grad_half, kl_part = divergence(
        teacher_tempered, student_tempered, teacher_lse, student_lse, token_factor
    )
    feature_count = student_head.shape[3]
    piece = lax.all_gather(student_head, "tok", axis=1, tiled=True)
    row_count = piece.shape[1] * piece.shape[2]
    partial_value = jnp.dot(
        grad_half, piece.reshape(row_count, feature_count), preferred_element_type=jnp.float32
    )
    summed = lax.psum(partial_value, ("vocab", "grp"))
    half_width = feature_count // 2
    hidden_grad = lax.dynamic_slice_in_dim(summed, group_index * half_width, half_width, 1)
    weighted_terms = jnp.sum(token_factor * kl_part)
    distill_loss_total = (
        lax.psum(weighted_terms, ("tok", "vocab", "grp"))
        * (SOFTEN_FACTOR * SOFTEN_FACTOR)
        / token_total_count
    )
    return (grad_half, hidden_grad, distill_loss_total)


def solution(mesh):
    placed = (P("grp", "tok", "vocab"), P("tok"), P("tok"), P(("vocab", "grp"), "tok", None, None))
    return jax.shard_map(
        per_device,
        mesh=mesh,
        in_specs=placed,
        out_specs=(P("tok", ("vocab", "grp")), P("tok", "grp"), P()),
        check_vma=False,
    )
```

profile of v0, /device:TPU:1, one launch (start us, length us, event | category | flops | bytes accessed | tf_op | source)
XLA Modules:
  0.0 336.0 jit_solution(1956912033627352121)
XLA Ops:
  7.2 0.0 all-gather.2.cloned.1.call-start
  7.2 0.7 all-gather.2.cloned.1.call-update
  7.9 3.2 copy.13
  11.1 2.8 copy.14
  13.9 0.0 copy-start
  13.9 5.0 %all-to-all-start = ((bf16[128,2,4096]{2,0,1:T(8,128)(2,1)}), bf16[128,2,4096]{2,0,1:T(8,128)(2,1)}, u32[]{:S(2)}, u32[]{:S(2)}) async-start(bf16[128,2,4096]{2,0,1:T(8,128)(2,1)} %copy.14), calls=%async_computation | async-start | bytes 4194304 | tf_op jit(solution)/shard_map/all_to_all | solution.py:52
  18.9 0.0 copy-start.1
  18.9 0.0 copy-start.2
  18.9 0.0 all-reduce.2.cloned.1.call-start
  18.9 0.0 copy-done
  19.0 0.5 fusion.2
  19.4 47.6 %pmax.7 = f32[128]{0:T(128)S(1)} all-reduce(f32[128]{0:T(128)S(1)} %fusion.2), channel_id=1, replica_groups=mesh['tok'=16,'vocab'=16,'grp'=2] {'vocab'}, use_global_device_ids=true, to_apply=%region_4.0 | all-reduce | flops 128 | bytes 1024 | tf_op jit(solution)/shard_map/pmax | solution.py:45
  67.1 5.2 %collective-permute-start = (f32[128]{0:T(128)S(1)}, f32[128]{0:T(128)S(1)}, u32[]{:S(2)}, u32[]{:S(2)}) collective-permute-start(f32[128]{0:T(128)S(1)} %pmax.7), channel_id=1, source_target_pairs={{0,1},{1,0},{2,3},{3,2},{4,5},{5,4},{6,7},{7,6},{8,9},{9,8},{10,11... | collective-permute-start | bytes 1544 | tf_op jit(solution)/shard_map/ppermute | solution.py:15
  72.3 0.0 copy-done.1
  72.3 1.0 fusion.1
  73.2 27.9 %psum.29 = f32[128]{0:T(128)S(1)} all-reduce(f32[128]{0:T(128)S(1)} %fusion.1), channel_id=1, replica_groups=mesh['tok'=16,'vocab'=16,'grp'=2] {'vocab'}, use_global_device_ids=true, to_apply=%region_6.0 | all-reduce | flops 128 | bytes 1024 | tf_op jit(solution)/shard_map/psum | solution.py:46
  101.1 0.0 copy-done.2
  101.1 0.1 select_reduce_fusion.1
  101.3 1.9 collective-permute-start.1
  103.2 33.1 %psum.28 = f32[8]{0:T(128)S(1)} all-reduce(f32[8]{0:T(128)S(1)} %select_reduce_fusion.1), channel_id=1, replica_groups=mesh['tok'=16,'vocab'=16,'grp'=2] {'tok'}, use_global_device_ids=true, to_apply=%region_1.0 | all-reduce | flops 8 | bytes 64 | tf_op jit(solution)/shard_map/psum | solution.py:41
  136.3 0.1 select_reduce_fusion
  136.4 0.0 collective-permute-done.1
  136.4 0.0 collective-permute-done
  136.4 0.0 all-to-all-done
  136.4 3.2 copy.15
  139.6 0.8 multiply_reduce_fusion
  140.4 0.6 multiply_reduce_fusion.1
  141.0 0.9 multiply_convert_fusion
  141.9 43.4 %all-gather.2.cloned.1.call-done = bf16[1,16,256,1792]{3,2,0,1:T(8,128)(2,1)} async-done(((bf16[1,1,256,1792]{3,2,0,1:T(8,128)(2,1)}), bf16[1,16,256,1792]{3,2,0,1:T(8,128)(2,1)}) %all-gather.2.cloned.1.call-update) | async-done | bytes 14680080 | tf_op jit(solution)/shard_map/all_gather | solution.py:59
  185.3 8.2 %fusion.4 = f32[128,1792]{1,0:T(8,128)} fusion(bf16[128,4096]{0,1:T(8,128)(2,1)S(1)} %multiply_convert_fusion, bf16[4096,1792]{1,0:T(8,128)(2,1)} %bitcast.12), kind=kOutput, calls=%fused_computation.21 | convolution fusion | flops 1879048192 | bytes 16646144 | tf_op jit(solution)/shard_map/dot_general | solution.py:61
  193.5 0.0 all-reduce.2.cloned.1.call-update
  193.5 103.2 %psum.31 = f32[]{:T(128)} all-reduce(f32[]{:T(128)} %get-tuple-element.9), channel_id=1, replica_groups=mesh['tok'=16,'vocab'=16,'grp'=2] {'tok','vocab','grp'}, use_global_device_ids=true, to_apply=%region_10.11 | all-reduce | flops 1 | bytes 8 | tf_op jit(solution)/shard_map/psum | solution.py:69
  296.7 1.3 copy.17
  298.7 27.5 %all-reduce.2.cloned.1.call-done = f32[128,1792]{1,0:T(8,128)} async-done(((f32[128,1792]{1,0:T(8,128)}), f32[128,1792]{1,0:T(8,128)}) %all-reduce.2.cloned.1.call-update) | async-done | bytes 917520 | tf_op jit(solution)/shard_map/psum | solution.py:64
  326.2 1.8 constant_dynamic-slice_fusion
  (3 shorter events, 0.0 us)
Async XLA Ops:
  7.2 178.1 %all-gather.2.cloned.1.call-start = ((), (), s32[]{:S(2)}) async-start(), calls=%async_computation.1 | async-start | bytes 15597568 | tf_op jit(solution)/shard_map/all_gather | solution.py:59
  13.9 5.0 %copy-start = (bf16[1,128,8192]{2,1,0:T(8,128)(2,1)S(1)}, bf16[1,128,8192]{2,1,0:T(8,128)(2,1)}, u32[]{:S(2)}) copy-start(bf16[1,128,8192]{2,1,0:T(8,128)(2,1)} %param.4) | copy-start | bytes 6291460
  13.9 122.5 %all-to-all-start = ((bf16[128,2,4096]{2,0,1:T(8,128)(2,1)}), bf16[128,2,4096]{2,0,1:T(8,128)(2,1)}, u32[]{:S(2)}, u32[]{:S(2)}) async-start(bf16[128,2,4096]{2,0,1:T(8,128)(2,1)} %copy.14), calls=%async_computation | async-start | bytes 4194304 | tf_op jit(solution)/shard_map/all_to_all | solution.py:52
  18.9 53.4 %copy-start.1 = (s32[128]{0:T(128)S(1)}, s32[128]{0:T(128)}, u32[]{:S(2)}) copy-start(s32[128]{0:T(128)} %param.6) | copy-start | bytes 1540
  18.9 82.3 %copy-start.2 = (s32[128]{0:T(128)S(1)}, s32[128]{0:T(128)}, u32[]{:S(2)}) copy-start(s32[128]{0:T(128)} %param.5) | copy-start | bytes 1540
  18.9 307.3 %all-reduce.2.cloned.1.call-start = ((), (), s32[]{:S(2)}) async-start(), calls=%async_computation.2 | async-start | bytes 1835008 | tf_op jit(solution)/shard_map/psum | solution.py:64
  67.1 69.3 %collective-permute-start = (f32[128]{0:T(128)S(1)}, f32[128]{0:T(128)S(1)}, u32[]{:S(2)}, u32[]{:S(2)}) collective-permute-start(f32[128]{0:T(128)S(1)} %pmax.7), channel_id=1, source_target_pairs={{0,1},{1,0},{2,3},{3,2},{4,5},{5,4},{6,7},{7,6},{8,9},{9,8},{10,11... | collective-permute-start | bytes 1544 | tf_op jit(solution)/shard_map/ppermute | solution.py:15
  101.3 35.1 %collective-permute-start.1 = (f32[128]{0:T(128)S(1)}, f32[128]{0:T(128)S(1)}, u32[]{:S(2)}, u32[]{:S(2)}) collective-permute-start(f32[128]{0:T(128)S(1)} %psum.29), channel_id=1, source_target_pairs={{0,1},{1,0},{2,3},{3,2},{4,5},{5,4},{6,7},{7,6},{8,9},{9,8},{10,11... | collective-permute-start | bytes 1544 | tf_op jit(solution)/shard_map/ppermute | solution.py:15
Sparse Core Ops, SparseCore 0:
  10.1 175.1 all-gather.1
  193.6 132.5 all-reduce.1
where the time goes:
time: 337 us; the launch traced here: 336 us
  blocking collectives  212 us (63%)
  waiting for transfers between devices  71.6 us (21%)
  between operations  15.9 us (5%)
  local copies, waits for them, and re-layouts  12.3 us (4%)
  starting transfers between devices  12.1 us (4%)
  matrix products  8.21 us (2%)
  other arithmetic  3.91 us (1%)
    psum x1, blocking collectives, per_device(): lax.psum(weighted_terms, ('tok', 'vocab', 'grp'))  103 us
    pmax x1, blocking collectives, per_device(): row_top = lax.pmax(jnp.max(tempered_logits, axis=1), 'vocab')  47.6 us
    all_gather x1, waiting for transfers between devices, per_device(): piece = lax.all_gather(student_head, 'tok', axis=1, tiled=True)  43.4 us
    psum x1, blocking collectives, per_device(): doc_sizes = lax.psum(local_counts, 'tok')  33.1 us
    psum x1, blocking collectives, per_device(): lax.psum(jnp.sum(jnp.exp(tempered_logits - row_top[:, None]), axis=1), 'v...  27.9 us
    psum x1, waiting for transfers between devices, per_device(): summed = lax.psum(partial_value, ('vocab', 'grp'))  27.5 us
    dot_general x1, matrix products, per_device(): jnp.dot(grad_half, piece.reshape(row_count, feature_count), preferred_ele...  8.21 us
    ppermute x2, starting transfers between devices, swapped(): return lax.ppermute(value, axis, pairs)  7.09 us
  transfers between devices with their start and end apart: 5, of which 2 were waited for; matrix products, arithmetic and copies ran while one was open for 4% of the time, Pallas kernels for 0%

commit v1 on v0

v1 whole, which is shorter than its diff:
```python
import functools

import jax
import jax.numpy as jnp
from jax import lax
from jax.experimental import pallas as pl
from jax.experimental.pallas import tpu as pltpu
from jax.sharding import PartitionSpec as P

SEGS = 8
SOFTEN = 2.0
NT = 16
ROWS = 128
HALF = 64
TH = 32
BLK = 256
COLS = 4096
HS = 1792
HH = 896
OFF = (0, 1, 7, 2, 6, 3, 5, 4)
MESH = pl.DeviceIdType.MESH
F32 = jnp.float32
BF16 = jnp.bfloat16


def kernel(
    lg_hbm, seg_ref, mask_ref, head_hbm,
    grad_out, hid_out, loss_out,
    lg, a_buf, gbuf, gnat, grx, hb, pb, rb, rsum, zs, zr, fb,
    sc, col, st, stc, sb, cz, cm, lz, lm, lp, lc,
    s_loc, x_s, x_r, h_s, h_r, c_s, c_r, t_s, t_r, g_s, g_r, o_s, o_r,
    p_s, p_r, z_s, z_r, f_s, f_r, l_s, l_r,
):
    z = lax.axis_index("tok")
    v = lax.axis_index("vocab")
    g = lax.axis_index("grp")
    c = v % 2
    xl = (v // 2) % 2
    y = v // 4
    j = v // 2
    par = z % 2
    oc = 1 - c
    og = 1 - g
    ov = v + 1 - 2 * c
    mate = (z + 1 + 14 * ((z + c) % 2)) % NT
    my_pos = (z + c) % 2

    def plane(r):
        h, a, b = r // 8, (r // 2) % 4, r % 2
        y2 = (y + 4 - a) % 4
        x2 = (xl + 2 - b) % 2
        g2 = (g + 2 - h) % 2
        return y2 * 2 + x2, g2, (z, y2 * 4 + x2 * 2 + c, g2)

    def column(p):
        return (z + NT - 2 * OFF[p]) % NT

    def send(src, dst, ss, rs, dev):
        copy = pltpu.make_async_remote_copy(
            src_ref=src, dst_ref=dst, send_sem=ss, recv_sem=rs, device_id=dev, device_id_type=MESH
        )
        copy.start()

    def wait(ref, sem):
        pltpu.make_async_copy(ref, ref, sem).wait()

    core_mate = (z, ov, g)

    in_logits = pltpu.make_async_copy(lg_hbm, lg, s_loc.at[0])
    in_logits.start()
    in_head = pltpu.make_async_copy(head_hbm, hb.at[c, my_pos], s_loc.at[1])
    in_head.start()
    mine = pl.ds(pl.multiple_of(HALF * c, HALF), HALF)
    own_cols = pl.ds(pl.multiple_of(COLS * g, COLS), COLS)
    in_own = pltpu.make_async_copy(lg_hbm.at[mine, own_cols], a_buf.at[g, c], s_loc.at[2])
    in_own.start()

    barrier = pltpu.get_barrier_semaphore()
    for dev in [core_mate, (z, ov, og), (mate, v, g)]:
        pl.semaphore_signal(barrier, inc=1, device_id=dev, device_id_type=MESH)
    for r in range(1, 16):
        pl.semaphore_signal(barrier, inc=1, device_id=plane(r)[2], device_id_type=MESH)
    for p in range(1, 8):
        pl.semaphore_signal(barrier, inc=1, device_id=(column(p), v, g), device_id_type=MESH)
    pl.semaphore_wait(barrier, 25)

    other_cols = pl.ds(pl.multiple_of(COLS * og, COLS), COLS)
    for th in range(2):
        dst = a_buf.at[g, c, pl.ds(TH * th, TH)]
        rows_same = pl.ds(pl.multiple_of(HALF * c + TH * th, TH), TH)
        rows_other = pl.ds(pl.multiple_of(HALF * oc + TH * th, TH), TH)
        send(lg_hbm.at[rows_same, other_cols], dst, x_s.at[th, 1], x_r.at[th, 1], (z, v, og))
        send(lg_hbm.at[rows_other, other_cols], dst, x_s.at[th, 2], x_r.at[th, 2], (z, ov, og))
        send(lg_hbm.at[rows_other, own_cols], dst, x_s.at[th, 0], x_r.at[th, 0], core_mate)

    docs = lax.broadcasted_iota(jnp.int32, (SEGS, ROWS), 0)
    member = (seg_ref[...] == docs).astype(F32)
    masked = mask_ref[...].astype(F32)
    cz[0] = member * masked
    for p in range(1, 8):
        send(cz.at[0], cz.at[p], c_s.at[0], c_r.at[0], (column(p), v, g))

    in_head.wait()
    send(hb.at[c, my_pos], hb.at[c, my_pos], h_s.at[0], h_r.at[0], (mate, v, g))
    send(hb.at[c, my_pos], hb.at[c, my_pos], h_s.at[1], h_r.at[1], core_mate)

    in_logits.wait()
    lane = lax.broadcasted_iota(jnp.int32, (16, 128), 1)

    def stat_rows(i, carry):
        rows = pl.ds(pl.multiple_of(i * 16, 16), 16)
        top = jnp.max(lg[rows, :].astype(F32), axis=1, keepdims=True) * (1.0 / SOFTEN)
        mass = jnp.sum(
            jnp.exp(lg[rows, :].astype(F32) * (1.0 / SOFTEN) - top), axis=1, keepdims=True
        )
        sc[rows, :] = jnp.where(lane == 0, top, mass)
        return carry

    lax.fori_loop(0, ROWS // 16, stat_rows, 0)
    st[0] = sc[...].T[:8]
    send(st.at[0], st.at[1], t_s.at[0], t_r.at[0], core_mate)

    wait(cz.at[pl.ds(1, 7)], c_r.at[0])
    part = cz[0]
    for p in range(1, 8):
        part = part + cz[p]
    cm[0] = part
    send(cm.at[0], cm.at[1], c_s.at[1], c_r.at[1], (mate, v, g))

    wait(st.at[1], t_r.at[0])
    top = jnp.maximum(st[0, 0:1, :], st[1, 0:1, :])
    mass = st[0, 1:2, :] * jnp.exp(st[0, 0:1, :] - top) + st[1, 1:2, :] * jnp.exp(st[1, 0:1, :] - top)
    sub = lax.broadcasted_iota(jnp.int32, (8, ROWS), 0)
    sb[0] = jnp.where(sub == 0, top, mass)
    for r in range(1, 16):
        send(sb.at[0], sb.at[r], t_s.at[1], t_r.at[1], plane(r)[2])

    wait(cm.at[1], c_r.at[1])
    sizes = jnp.sum(cm[0] + cm[1], axis=1, keepdims=True)
    own_size = jnp.sum(member * sizes, axis=0, keepdims=True)
    weight = masked * (NT * ROWS // SEGS) / own_size

    wait(sb.at[pl.ds(1, 15)], t_r.at[1])

    def lse(first):
        top = sb[first, 0:1, :]
        for r in range(first + 1, first + 8):
            top = jnp.maximum(top, sb[r, 0:1, :])
        mass = jnp.zeros_like(top)
        for r in range(first, first + 8):
            mass = mass + sb[r, 1:2, :] * jnp.exp(sb[r, 0:1, :] - top)
        return top + jnp.log(mass)

    own_lse, other_lse = lse(0), lse(8)
    teacher_lse = jnp.where(g == 0, own_lse, other_lse)
    student_lse = jnp.where(g == 0, other_lse, own_lse)
    sc[...] = jnp.zeros_like(sc)
    sc[0:8, :] = jnp.where(sub == 0, teacher_lse, jnp.where(sub == 1, student_lse, weight))
    col[...] = sc[...].T

    loss_acc = jnp.zeros((TH, 128), F32)
    for th in range(2):
        if th == 0:
            in_own.wait()
        wait(a_buf.at[g, oc, pl.ds(TH * th, TH)], x_r.at[th, 0])
        wait(a_buf.at[og, c, pl.ds(TH * th, TH)], x_r.at[th, 1])
        wait(a_buf.at[og, oc, pl.ds(TH * th, TH)], x_r.at[th, 2])
        rows = pl.ds(TH * th, TH)
        stats = col[pl.ds(pl.multiple_of(HALF * c + TH * th, TH), TH), :]
        t_lse, s_lse, wgt = stats[:, 0:1], stats[:, 1:2], stats[:, 2:3]
        scale = SOFTEN * wgt
        for p in list(range(1, 8)) + [0]:
            i = (z // 2 + 8 - OFF[p]) % 8
            blocks = (
                (0, 2 * i),
                (0, 2 * i + 1),
                (1, (2 * i + 15 + 2 * par) % 16),
                (1, (2 * i + 2 * par) % 16),
            )
            for kb, (b, k) in enumerate(blocks):
                cols = pl.ds(pl.multiple_of(BLK * k, BLK), BLK)
                log_t = a_buf[0, b, rows, cols].astype(F32) * (1.0 / SOFTEN) - t_lse
                log_s = a_buf[1, b, rows, cols].astype(F32) * (1.0 / SOFTEN) - s_lse
                prob_t = jnp.exp(log_t)
                prob_s = jnp.exp(log_s)
                grad = (scale * (prob_s - prob_t)).astype(BF16)
                term = prob_t * (log_t - log_s)
                loss_acc = loss_acc + wgt * (term[:, :128] + term[:, 128:])
                gnat[b, rows, cols] = grad
                if p == 0:
                    grx[th, 0, :, kb * BLK:(kb + 1) * BLK] = grad
                else:
                    gbuf[th, p, :, kb * BLK:(kb + 1) * BLK] = grad
            if p:
                send(gbuf.at[th, p], grx.at[th, p], g_s.at[th], g_r.at[th, p // 4], (column(p), v, g))

    out_own = pltpu.make_async_copy(gnat.at[c], grad_out.at[mine, :], s_loc.at[3])
    out_own.start()
    send(gnat.at[oc], grad_out.at[mine, :], o_s, o_r, core_mate)

    lz[0] = loss_acc[0:8] + loss_acc[8:16] + loss_acc[16:24] + loss_acc[24:32]
    for p in range(1, 8):
        send(lz.at[0], lz.at[p], l_s.at[0], l_r.at[0], (column(p), v, g))

    wait(hb.at[c, 1 - my_pos], h_r.at[0])
    send(hb.at[c, 1 - my_pos], hb.at[c, 1 - my_pos], h_s.at[2], h_r.at[2], core_mate)
    wait(hb.at[oc, (z + oc) % 2], h_r.at[1])
    wait(hb.at[oc, 1 - (z + oc) % 2], h_r.at[2])

    out_row = lax.broadcasted_iota(jnp.int32, (128, 128), 0)
    in_row = lax.broadcasted_iota(jnp.int32, (128, 128), 1)
    source = ((out_row // 4) % 4) * TH + (out_row // 16) * 4 + out_row % 4
    order = (in_row == source).astype(F32).astype(BF16)

    def multiply(q):
        th, bh = q // 2, q % 2
        if bh == 0:
            wait(grx.at[th, pl.ds(1, 3)], g_r.at[th, 0])
        else:
            wait(grx.at[th, pl.ds(4, 4)], g_r.at[th, 1])
        x = grx[th, 4 * bh:4 * bh + 4].reshape(128, 4 * BLK)
        x = jnp.dot(order, x, preferred_element_type=F32).astype(BF16)
        for gg in range(2):
            part = jnp.dot(
                x[:, :512], hb[0, :, :, HH * gg:HH * gg + HH].reshape(512, HH), preferred_element_type=F32
            ) + jnp.dot(
                x[:, 512:], hb[1, :, :, HH * gg:HH * gg + HH].reshape(512, HH), preferred_element_type=F32
            )
            pb[q, gg] = part.astype(BF16).reshape(8, 16, HH)
        for r in range(1, 16):
            j2, g2, dev = plane(r)
            send(pb.at[q, g2, j2], rb.at[q, r], p_s.at[q], p_r.at[q], dev)

    def reduce(q):
        wait(rb.at[q, pl.ds(1, 15)], p_r.at[q])
        total = pb[q, g, j].astype(F32)
        for r in range(1, 16):
            total = total + rb[q, r].astype(F32)
        rsum[q] = total

    def spread(bh):
        for bb in range(4):
            p = 4 * bh + bb
            zs[p] = jnp.concatenate([rsum[bh, 4 * bb:4 * bb + 4], rsum[2 + bh, 4 * bb:4 * bb + 4]], axis=0)
            if p:
                dev = ((z + 2 * OFF[p]) % NT, v, g)
                send(zs.at[p], zr.at[p], z_s.at[bh], z_r.at[bh], dev)

    multiply(0)
    wait(lz.at[pl.ds(1, 7)], l_r.at[0])
    part = lz[0]
    for p in range(1, 8):
        part = part + lz[p]
    lm[0] = part
    send(lm.at[0], lm.at[1], l_s.at[1], l_r.at[1], (mate, v, g))
    multiply(1)
    reduce(0)
    wait(lm.at[1], l_r.at[1])
    lp[0] = lm[0] + lm[1]
    for r in range(1, 16):
        send(lp.at[0], lp.at[r], l_s.at[2], l_r.at[2], plane(r)[2])
    multiply(2)
    reduce(1)
    wait(lp.at[pl.ds(1, 15)], l_r.at[2])
    part = lp[0]
    for r in range(1, 16):
        part = part + lp[r]
    lc[0] = part
    send(lc.at[0], lc.at[1], l_s.at[3], l_r.at[3], core_mate)
    multiply(3)
    reduce(2)
    spread(0)
    wait(lc.at[1], l_r.at[3])
    loss_out[...] = (
        jnp.sum(lc[0] + lc[1], keepdims=True) * (SOFTEN * SOFTEN) / (NT * ROWS)
    )
    reduce(3)
    spread(1)

    wait(zr.at[pl.ds(1, 3)], z_r.at[0])
    wait(zr.at[pl.ds(4, 4)], z_r.at[1])
    total = zs[0]
    for p in range(1, 8):
        total = total + zr[p]
    fb[j] = total
    for r in range(1, 8):
        send(fb.at[j], fb.at[j], f_s.at[0], f_r.at[0], plane(r)[2])
    wait(fb.at[pl.ds(0, 7)], f_r.at[0])
    for th in range(2):
        for jj in range(4):
            rows = pl.ds(pl.multiple_of(HALF * c + TH * th + 8 * jj, 8), 8)
            hid_out[rows, :] = jnp.concatenate(
                [fb[2 * jj, 4 * th:4 * th + 4], fb[2 * jj + 1, 4 * th:4 * th + 4]], axis=0
            )
    send(hid_out.at[mine, :], hid_out.at[mine, :], f_s.at[1], f_r.at[1], core_mate)

    for th in range(2):
        for k in range(3):
            wait(a_buf.at[0, 0, pl.ds(0, TH)], x_s.at[th, k])
        wait(grx.at[th, pl.ds(1, 7)], g_s.at[th])
    for k in range(3):
        wait(hb.at[0, 0], h_s.at[k])
    wait(cz.at[pl.ds(1, 7)], c_s.at[0])
    wait(cm.at[1], c_s.at[1])
    wait(st.at[1], t_s.at[0])
    wait(sb.at[pl.ds(1, 15)], t_s.at[1])
    out_own.wait()
    wait(gnat.at[0], o_s)
    wait(grad_out.at[pl.ds(pl.multiple_of(HALF * oc, HALF), HALF), :], o_r)
    for q in range(4):
        wait(rb.at[q, pl.ds(1, 15)], p_s.at[q])
    wait(zr.at[pl.ds(1, 3)], z_s.at[0])
    wait(zr.at[pl.ds(4, 4)], z_s.at[1])
    wait(fb.at[pl.ds(0, 7)], f_s.at[0])
    wait(lz.at[pl.ds(1, 7)], l_s.at[0])
    wait(lm.at[1], l_s.at[1])
    wait(lp.at[pl.ds(1, 15)], l_s.at[2])
    wait(lc.at[1], l_s.at[3])
    wait(hid_out.at[mine, :], f_s.at[1])
    wait(hid_out.at[pl.ds(pl.multiple_of(HALF * oc, HALF), HALF), :], f_r.at[1])


def per_device(logits, segment_ids, token_mask, student_head):
    dma = pltpu.SemaphoreType.DMA
    any_space = pl.BlockSpec(memory_space=pl.ANY)
    vmem_space = pl.BlockSpec(memory_space=pltpu.VMEM)
    grad, hidden, loss = pl.pallas_call(
        kernel,
        out_shape=(
            jax.ShapeDtypeStruct((ROWS, COLS), BF16),
            jax.ShapeDtypeStruct((ROWS, HH), F32),
            jax.ShapeDtypeStruct((1, 1), F32),
        ),
        in_specs=[any_space, vmem_space, vmem_space, any_space],
        out_specs=(any_space, vmem_space, vmem_space),
        scratch_shapes=[
            pltpu.VMEM((ROWS, 2 * COLS), BF16),
            pltpu.VMEM((2, 2, HALF, COLS), BF16),
            pltpu.VMEM((2, 8, TH, 4 * BLK), BF16),
            pltpu.VMEM((2, HALF, COLS), BF16),
            pltpu.VMEM((2, 8, TH, 4 * BLK), BF16),
            pltpu.VMEM((2, 2, BLK, HS), BF16),
            pltpu.VMEM((4, 2, 8, 16, HH), BF16),
            pltpu.VMEM((4, 16, 16, HH), BF16),
            pltpu.VMEM((4, 16, HH), F32),
            pltpu.VMEM((8, 8, HH), F32),
            pltpu.VMEM((8, 8, HH), F32),
            pltpu.VMEM((8, 8, HH), F32),
            pltpu.VMEM((128, 128), F32),
            pltpu.VMEM((128, 128), F32),
            pltpu.VMEM((2, 8, 128), F32),
            pltpu.VMEM((2, 8, 128), F32),
            pltpu.VMEM((16, 8, 128), F32),
            pltpu.VMEM((8, 8, 128), F32),
            pltpu.VMEM((2, 8, 128), F32),
            pltpu.VMEM((8, 8, 128), F32),
            pltpu.VMEM((2, 8, 128), F32),
            pltpu.VMEM((16, 8, 128), F32),
            pltpu.VMEM((2, 8, 128), F32),
            dma((4,)),
            dma((2, 3)), dma((2, 3)),
            dma((3,)), dma((3,)),
            dma((2,)), dma((2,)),
            dma((2,)), dma((2,)),
            dma((2,)), dma((2, 2)),
            dma, dma,
            dma((4,)), dma((4,)),
            dma((2,)), dma((2,)),
            dma((2,)), dma((2,)),
            dma((4,)), dma((4,)),
        ],
        compiler_params=pltpu.CompilerParams(
            collective_id=0, has_side_effects=True, vmem_limit_bytes=40 * 1024 * 1024
        ),
        cost_estimate=pl.CostEstimate(
            flops=2 * ROWS * COLS * HS, bytes_accessed=6 * 1024 * 1024, transcendentals=3 * ROWS * COLS
        ),
        name="distill",
    )(
        logits.reshape(ROWS, 2 * COLS),
        segment_ids.reshape(1, ROWS),
        token_mask.reshape(1, ROWS),
        student_head.reshape(BLK, HS),
    )
    return grad, hidden, loss.reshape(())


def solution(mesh):
    placed = (P("grp", "tok", "vocab"), P("tok"), P("tok"), P(("vocab", "grp"), "tok", None, None))
    return jax.shard_map(
        per_device,
        mesh=mesh,
        in_specs=placed,
        out_specs=(P("tok", ("vocab", "grp")), P("tok", "grp"), P()),
        check_vma=False,
    )
```

time: 337 us -> 141 us (0.42)
  blocking collectives: 212 us -> 0 us
  Pallas kernels: 0 us -> 132 us
  waiting for transfers between devices: 71.6 us -> 0 us
  between operations: 15.9 us -> 2.4 us
  starting transfers between devices: 12.1 us -> 0 us
  matrix products: 8.21 us -> 0 us
  local copies, waits for them, and re-layouts: 12.3 us -> 5.81 us
  other arithmetic: 3.91 us -> 0 us
    psum x3 -> x0, blocking collectives: 164 us -> none  [the longest x1 103 us: per_device(): lax.psum(weighted_terms, ('tok', 'vocab', 'grp'))]
    pallas_call x0 -> x1, Pallas kernels: none -> 132 us  [per_device(): pl.pallas_call(kernel, out_shape=(jax.ShapeDtypeStruct((ROWS, COLS), BF16...]
    pmax x1 -> x0, blocking collectives: 47.6 us -> none  [per_device(): row_top = lax.pmax(jnp.max(tempered_logits, axis=1), 'vocab')]
    all_gather x1 -> x0, waiting for transfers between devices: 43.4 us -> none  [per_device(): piece = lax.all_gather(student_head, 'tok', axis=1, tiled=True)]
    psum x1 -> x0, waiting for transfers between devices: 27.5 us -> none  [per_device(): summed = lax.psum(partial_value, ('vocab', 'grp'))]
    dot_general x1 -> x0, matrix products: 8.21 us -> none  [per_device(): jnp.dot(grad_half, piece.reshape(row_count, feature_count), preferred_ele...]
    ppermute x2 -> x0, starting transfers between devices: 7.09 us -> none  [swapped(): return lax.ppermute(value, axis, pairs)]
    all_to_all x2 -> x0, local copies, waits for them, and re-layouts: 5.96 us -> none  [per_device(): lax.all_to_all(resident_tile, 'grp', split_axis=1, concat_axis=1, tiled=T...]
  transfers between devices with their start and end apart: 5 -> 0, of which waited for: 2 -> 0; matrix products, arithmetic and copies ran while one was open for 4% -> 0% of each run, Pallas kernels for 0% -> 0%
where the time goes in v1:
time: 141 us; the launch traced here: 140 us
  Pallas kernels  132 us (94%)
  local copies, waits for them, and re-layouts  5.81 us (4%)
  between operations  2.4 us (2%)
    pallas_call x1, Pallas kernels, per_device(): pl.pallas_call(kernel, out_shape=(jax.ShapeDtypeStruct((ROWS, COLS), BF16...  132 us
    unnamed x10, local copies, waits for them, and re-layouts  5.81 us

profile of v1, /device:TPU:1, one launch (start us, length us, event | category | flops | bytes accessed | tf_op | source)
XLA Modules:
  0.0 140.4 jit_solution(15435965888031419979)
XLA Ops:
  0.6 0.0 copy-start
  0.6 1.6 %copy-done = bf16[1,128,8192]{2,1,0:T(8,128)(2,1)S(1)} copy-done((bf16[1,128,8192]{2,1,0:T(8,128)(2,1)S(1)}, bf16[1,128,8192]{2,1,0:T(8,128)(2,1)}, u32[]{:S(2)}) %copy-start) | copy-done | bytes 2097176
  2.2 0.0 copy-start.1
  2.2 1.2 copy-done.1
  3.4 0.0 copy-start.2
  3.4 0.7 copy-done.2
  4.1 0.0 copy-start.3
  4.1 0.7 copy-done.3
  4.7 132.2 %distill.1 = (bf16[128,4096]{1,0:T(8,128)(2,1)S(1)}, f32[128,896]{1,0:T(8,128)S(1)}, f32[1,1]{1,0:T(1,128)}) custom-call(bf16[128,8192]{1,0:T(8,128)(2,1)S(1)} %bitcast.5, s32[1,128]{1,0:T(1,128)S(1)} %bitcast.7, s32[1,128]{1,0:T(1,128)S(1)} %bitcast.8, bf16[256,1792]{1,0:T(8,128)(2,1)S(1)} %bitcast.6), custom_call_target="tpu_custom_call" | custom-call | flops 1879048192 | bytes 6291456 | tf_op jit(solution)/shard_map/distill/pallas_call | solution.py:327
  136.9 1.0 copy.10
  137.9 0.8 copy.11
Async XLA Ops:
  0.6 1.6 %copy-start = (bf16[1,128,8192]{2,1,0:T(8,128)(2,1)S(1)}, bf16[1,128,8192]{2,1,0:T(8,128)(2,1)}, u32[]{:S(2)}) copy-start(bf16[1,128,8192]{2,1,0:T(8,128)(2,1)} %param.4) | copy-start | bytes 6291460
  2.2 1.2 copy-start.1
  3.4 0.7 copy-start.2
  4.1 0.7 copy-start.3

commit v2 on v1

v2 whole, which is shorter than its diff:
```python
import jax
import jax.numpy as jnp
from jax import lax
from jax.experimental import pallas as pl
from jax.experimental.pallas import tpu as pltpu
from jax.sharding import PartitionSpec as P

SEGS = 8
SOFTEN = 2.0
NT = 16
ROWS = 128
HALF = 64
TH = 32
BLK = 256
COLS = 4096
HS = 1792
HH = 896
VMEM_BYTES = 54 * 1024 * 1024
MESH = pl.DeviceIdType.MESH
F32 = jnp.float32
BF16 = jnp.bfloat16
LAST = 7


def off(p):
    return (4 + ((p + 1) // 2) * (1 - 2 * (p % 2))) % 8


def kernel(
    lg_hbm, seg_hbm, mask_hbm, head_hbm,
    grad_out, hid_out, loss_out,
    lg, ao, gb, gn, grx, hb, pb, rb, rsum, zs, zr, own, fb,
    sc, col, st, sb, cz, cm, acc, lz, lm, lp, lc, seg_ref, mask_ref,
    s_loc, x_s, x_r, h_s, h_r, c_s, c_r, t_s, t_r, g_s, g_r,
    p_s, p_r, z_s, z_r, f_s, f_r, l_s, l_r,
):
    z = lax.axis_index("tok")
    v = lax.axis_index("vocab")
    g = lax.axis_index("grp")
    c = v % 2
    xl = (v // 2) % 2
    y = v // 4
    j = v // 2
    par = z % 2
    oc = 1 - c
    og = 1 - g
    ov = v + 1 - 2 * c
    mate = (z + 1 + 14 * ((z + c) % 2)) % NT
    my_pos = (z + c) % 2

    def plane(r):
        h, a, b = r // 8, (r // 2) % 4, r % 2
        y2 = (y + 4 - a) % 4
        x2 = (xl + 2 - b) % 2
        g2 = (g + 2 - h) % 2
        return y2 * 2 + x2, g2

    def plane_dev(r, core):
        j2, g2 = plane(r)
        return (z, j2 * 2 + core, g2)

    def column(p):
        return (z + NT - 2 * off(p)) % NT

    def send(src, dst, ss, rs, dev):
        copy = pltpu.make_async_remote_copy(
            src_ref=src, dst_ref=dst, send_sem=ss, recv_sem=rs, device_id=dev, device_id_type=MESH
        )
        copy.start()

    def wait(ref, sem):
        pltpu.make_async_copy(ref, ref, sem).wait()

    def loop(first, last, body):
        def step(i, carry):
            body(i)
            return carry

        lax.fori_loop(first, last, step, 0)

    core_mate = (z, ov, g)

    in_logits = pltpu.make_async_copy(lg_hbm, lg, s_loc.at[0])
    in_logits.start()
    in_head = pltpu.make_async_copy(head_hbm, hb.at[c, my_pos], s_loc.at[1])
    in_head.start()
    in_seg = pltpu.make_async_copy(seg_hbm, seg_ref, s_loc.at[2])
    in_seg.start()
    in_mask = pltpu.make_async_copy(mask_hbm, mask_ref, s_loc.at[3])
    in_mask.start()

    barrier = pltpu.get_barrier_semaphore()

    def greet(dev):
        pl.semaphore_signal(barrier, inc=1, device_id=dev, device_id_type=MESH)

    greet((mate, v, g))
    loop(1, 16, lambda r: greet(plane_dev(r, c)))
    loop(0, 8, lambda r: greet(plane_dev(r, oc)))

    def greet_column(p):
        greet((column(p), v, g))
        greet((column(p), ov, g))

    loop(0, LAST, greet_column)

    in_logits.wait()
    lane = lax.broadcasted_iota(jnp.int32, (16, 128), 1)

    def stat_rows(i):
        rows = pl.ds(pl.multiple_of(i * 16, 16), 16)
        top = jnp.max(lg[rows, :].astype(F32), axis=1, keepdims=True) * (1.0 / SOFTEN)
        mass = jnp.sum(
            jnp.exp(lg[rows, :].astype(F32) * (1.0 / SOFTEN) - top), axis=1, keepdims=True
        )
        sc[rows, :] = jnp.where(lane == 0, top, mass)

    loop(0, ROWS // 16, stat_rows)
    st[0] = sc[...].T[:8]
    pl.semaphore_wait(barrier, 38)

    other_cols = pl.ds(pl.multiple_of(COLS * og, COLS), COLS)

    def exchange(t):
        rows = pl.ds(TH * t, TH)
        send(lg_hbm.at[rows, other_cols], ao.at[rows], x_s.at[t], x_r.at[t], (z, v, og))

    send(st.at[0], st.at[1], t_s.at[0], t_r.at[0], core_mate)
    exchange(0)
    exchange(1)

    in_seg.wait()
    in_mask.wait()
    docs = lax.broadcasted_iota(jnp.int32, (SEGS, ROWS), 0)
    member = (seg_ref[...] == docs).astype(F32)
    masked = mask_ref[...].astype(F32)
    cz[LAST] = member * masked
    loop(0, LAST, lambda p: send(cz.at[LAST], cz.at[p], c_s.at[0], c_r.at[0], (column(p), v, g)))

    in_head.wait()
    send(hb.at[c, my_pos], hb.at[c, my_pos], h_s.at[0], h_r.at[0], (mate, v, g))
    send(hb.at[c, my_pos], hb.at[c, my_pos], h_s.at[1], h_r.at[1], core_mate)


    wait(st.at[1], t_r.at[0])
    top = jnp.maximum(st[0, 0:1, :], st[1, 0:1, :])
    mass = st[0, 1:2, :] * jnp.exp(st[0, 0:1, :] - top) + st[1, 1:2, :] * jnp.exp(st[1, 0:1, :] - top)
    sub = lax.broadcasted_iota(jnp.int32, (8, ROWS), 0)
    sb[0] = jnp.where(sub == 0, top, mass)
    loop(1, 16, lambda r: send(sb.at[0], sb.at[r], t_s.at[1], t_r.at[1], plane_dev(r, c)))
    exchange(2)

    wait(cz.at[pl.ds(0, LAST)], c_r.at[0])
    part = cz[0]
    for p in range(1, 8):
        part = part + cz[p]
    cm[0] = part
    send(cm.at[0], cm.at[1], c_s.at[1], c_r.at[1], (mate, v, g))
    exchange(3)

    wait(cm.at[1], c_r.at[1])
    sizes = jnp.sum(cm[0] + cm[1], axis=1, keepdims=True)
    own_size = jnp.sum(member * sizes, axis=0, keepdims=True)
    weight = masked * (NT * ROWS // SEGS) / own_size
    acc[...] = jnp.zeros_like(acc)

    wait(sb.at[pl.ds(1, 15)], t_r.at[1])

    def lse(first):
        top = sb[first, 0:1, :]
        for r in range(first + 1, first + 8):
            top = jnp.maximum(top, sb[r, 0:1, :])
        mass = jnp.zeros_like(top)
        for r in range(first, first + 8):
            mass = mass + sb[r, 1:2, :] * jnp.exp(sb[r, 0:1, :] - top)
        return top + jnp.log(mass)

    own_lse, other_lse = lse(0), lse(8)
    sc[...] = jnp.zeros_like(sc)
    sc[0:8, :] = jnp.where(sub == 0, own_lse, jnp.where(sub == 1, other_lse, weight))
    col[...] = sc[...].T

    sign = jnp.where(g == 0, -1.0, 1.0).astype(F32)

    def block(t, p):
        i = (z // 2 + 8 - off(p)) % 8
        first = (2 * i + c * (15 + 2 * par)) % 16
        rows = pl.ds(pl.multiple_of(TH * t, TH), TH)
        stats = col[rows, :]
        own_l, other_l, wgt = stats[:, 0:1], stats[:, 1:2], stats[:, 2:3]
        scale = (SOFTEN * sign) * wgt
        for n, k in enumerate((first, (first + 1) % 16)):
            cols = pl.ds(pl.multiple_of(BLK * k, BLK), BLK)
            own_at = pl.ds(pl.multiple_of(COLS * g + BLK * k, BLK), BLK)
            log_own = lg[rows, own_at].astype(F32) * (1.0 / SOFTEN) - own_l
            log_other = ao[rows, cols].astype(F32) * (1.0 / SOFTEN) - other_l
            p_own = jnp.exp(log_own)
            p_other = jnp.exp(log_other)
            grad = (scale * (p_own - p_other)).astype(BF16)
            term = jnp.where(g == 0, p_own, p_other) * (log_own - log_other)
            acc[...] += wgt * (term[:, :128] + term[:, 128:])
            gn[rows, cols] = grad
            gb[p, rows, BLK * n:BLK * n + BLK] = grad

    def chunk(t):
        wait(ao.at[pl.ds(pl.multiple_of(TH * t, TH), TH)], x_r.at[t])
        there = pl.ds(pl.multiple_of(16 * t, 16), 16)

        def place(p):
            block(t, p)
            for e in range(2):
                here = pl.ds(pl.multiple_of(TH * t + 16 * e, 16), 16)
                send(
                    gb.at[p, here], grx.at[c, p, there], g_s.at[0], g_r.at[2 * (t // 2) + p // 4],
                    (column(p), 2 * j + e, g),
                )

        loop(0, LAST, place)
        block(t, LAST)
        mine = pl.ds(pl.multiple_of(TH * t + 16 * c, 16), 16)
        theirs = pl.ds(pl.multiple_of(TH * t + 16 * oc, 16), 16)
        grx[c, LAST, there, :] = gb[LAST, mine, :]
        send(gb.at[LAST, theirs], grx.at[c, LAST, there], g_s.at[1], g_r.at[4 + t // 2], core_mate)

    loop(0, 4, chunk)

    out_own = pltpu.make_async_copy(gn, grad_out, s_loc.at[4])
    out_own.start()

    lp[0] = (acc[0:8] + acc[8:16] + acc[16:24] + acc[24:32]) * (-sign)
    loop(1, 16, lambda r: send(lp.at[0], lp.at[r], l_s.at[2], l_r.at[2], plane_dev(r, c)))

    wait(hb.at[c, 1 - my_pos], h_r.at[0])
    send(hb.at[c, 1 - my_pos], hb.at[c, 1 - my_pos], h_s.at[2], h_r.at[2], core_mate)

    out_row = lax.broadcasted_iota(jnp.int32, (128, 128), 0)
    in_row = lax.broadcasted_iota(jnp.int32, (128, 128), 1)
    source = ((out_row // 4) % 4) * TH + (out_row // 16) * 4 + out_row % 4
    order = (in_row == source).astype(F32).astype(BF16)

    wait(hb.at[oc, (z + oc) % 2], h_r.at[1])
    wait(hb.at[oc, 1 - (z + oc) % 2], h_r.at[2])

    def loss_plane():
        wait(lp.at[pl.ds(1, 15)], l_r.at[2])
        part = lp[0]
        for r in range(1, 16):
            part = part + lp[r]
        lc[0] = part
        send(lc.at[0], lc.at[1], l_s.at[3], l_r.at[3], core_mate)

    def reduce(q):
        wait(rb.at[q, pl.ds(1, 15)], p_r.at[q])
        total = pb[q, g, j].astype(F32)
        for r in range(1, 16):
            total = total + rb[q, r].astype(F32)
        rsum[q] = total

    def multiply(q):
        th, bh = q // 2, q % 2
        rows = pl.ds(pl.multiple_of(TH * th, TH), TH)

        @pl.when(bh == 0)
        def _():
            wait(grx.at[:, pl.ds(0, 4), rows], g_r.at[2 * th])

        @pl.when(bh == 1)
        def _():
            wait(grx.at[:, pl.ds(4, 3), rows], g_r.at[2 * th + 1])
            wait(grx.at[oc, LAST, rows], g_r.at[4 + th])

        xs = []
        for b in range(2):
            x = grx[b, pl.ds(4 * bh, 4), rows, :].reshape(128, 2 * BLK)
            xs.append(jnp.dot(order, x, preferred_element_type=F32).astype(BF16))
        for gg in range(2):
            part = jnp.dot(
                xs[0], hb[0, :, :, HH * gg:HH * gg + HH].reshape(512, HH), preferred_element_type=F32
            ) + jnp.dot(
                xs[1], hb[1, :, :, HH * gg:HH * gg + HH].reshape(512, HH), preferred_element_type=F32
            )
            pb[q, gg] = part.astype(BF16).reshape(8, 16, HH)

        def share(r):
            j2, g2 = plane(r)
            send(pb.at[q, g2, j2], rb.at[q, r], p_s.at[q], p_r.at[q], (z, j2 * 2 + c, g2))

        loop(1, 16, share)

        @pl.when(q > 0)
        def _():
            reduce(q - 1)

        pl.when(q == 1)(loss_plane)

    def spread(bh):
        for bb in range(4):
            p = 4 * bh + bb
            x = jnp.concatenate([rsum[bh, 4 * bb:4 * bb + 4], rsum[2 + bh, 4 * bb:4 * bb + 4]], axis=0)
            x = jnp.concatenate([x[:, :512], jnp.pad(x[:, 512:], ((0, 0), (0, 128)))], axis=0)
            if p == LAST:
                own[...] = x
            else:
                zs[p] = x.astype(BF16)
                send(zs.at[p], zr.at[p], z_s.at[bh], z_r.at[bh], ((z + 2 * off(p)) % NT, v, g))

    loop(0, 4, multiply)
    spread(0)
    wait(lc.at[1], l_r.at[3])
    lz[LAST] = lc[0] + lc[1]
    loop(0, LAST, lambda p: send(lz.at[LAST], lz.at[p], l_s.at[0], l_r.at[0], (column(p), v, g)))
    reduce(3)
    spread(1)

    wait(zr.at[pl.ds(0, 4)], z_r.at[0])
    wait(zr.at[pl.ds(4, 3)], z_r.at[1])
    total = own[...]
    for p in range(LAST):
        total = total + zr[p].astype(F32)
    slot = 8 * c + j
    fb[slot] = jnp.concatenate([total[:8], total[8:, :384]], axis=1)
    loop(1, 8, lambda r: send(fb.at[slot], fb.at[slot], f_s, f_r, plane_dev(r, c)))
    loop(0, 8, lambda r: send(fb.at[slot], fb.at[slot], f_s, f_r, plane_dev(r, oc)))

    wait(lz.at[pl.ds(0, LAST)], l_r.at[0])
    part = lz[0]
    for p in range(1, 8):
        part = part + lz[p]
    lm[0] = part
    send(lm.at[0], lm.at[1], l_s.at[1], l_r.at[1], (mate, v, g))

    loop(0, 4, lambda t: wait(ao.at[pl.ds(0, TH)], x_s.at[t]))
    wait(grx.at[:, pl.ds(0, LAST)], g_s.at[0])
    wait(grx.at[0, LAST], g_s.at[1])
    loop(0, 3, lambda k: wait(hb.at[0, 0], h_s.at[k]))
    wait(cz.at[pl.ds(0, LAST)], c_s.at[0])
    wait(cm.at[1], c_s.at[1])
    wait(st.at[1], t_s.at[0])
    wait(sb.at[pl.ds(1, 15)], t_s.at[1])
    out_own.wait()
    loop(0, 4, lambda q: wait(rb.at[q, pl.ds(1, 15)], p_s.at[q]))
    wait(zr.at[pl.ds(0, 4)], z_s.at[0])
    wait(zr.at[pl.ds(4, 3)], z_s.at[1])
    wait(lz.at[pl.ds(0, LAST)], l_s.at[0])
    wait(lm.at[1], l_s.at[1])
    wait(lp.at[pl.ds(1, 15)], l_s.at[2])
    wait(lc.at[1], l_s.at[3])
    wait(lm.at[1], l_r.at[1])
    loss_out[...] = jnp.sum(lm[0] + lm[1], keepdims=True) * (SOFTEN * SOFTEN) / (NT * ROWS)

    wait(fb.at[pl.ds(0, 15)], f_r)
    for t in range(4):
        for e in range(2):
            for h in range(2):
                n = 8 * e + 4 * (t % 2) + 2 * h
                at = 4 * (t // 2)
                row = TH * t + 16 * e + 8 * h
                hid_out[row:row + 8, :] = jnp.concatenate(
                    [fb[n, at:at + 4], fb[n + 1, at:at + 4]], axis=0
                )
    wait(fb.at[pl.ds(0, 15)], f_s)


def per_device(logits, segment_ids, token_mask, student_head):
    dma = pltpu.SemaphoreType.DMA
    any_space = pl.BlockSpec(memory_space=pl.ANY)
    vmem_space = pl.BlockSpec(memory_space=pltpu.VMEM)
    grad, hidden, loss = pl.pallas_call(
        kernel,
        out_shape=(
            jax.ShapeDtypeStruct((ROWS, COLS), BF16),
            jax.ShapeDtypeStruct((ROWS, HH), F32),
            jax.ShapeDtypeStruct((1, 1), F32),
        ),
        in_specs=[any_space] * 4,
        out_specs=(any_space, vmem_space, vmem_space),
        scratch_shapes=[
            pltpu.VMEM((ROWS, 2 * COLS), BF16),
            pltpu.VMEM((ROWS, COLS), BF16),
            pltpu.VMEM((8, ROWS, 2 * BLK), BF16),
            pltpu.VMEM((ROWS, COLS), BF16),
            pltpu.VMEM((2, 8, HALF, 2 * BLK), BF16),
            pltpu.VMEM((2, 2, BLK, HS), BF16),
            pltpu.VMEM((4, 2, 8, 16, HH), BF16),
            pltpu.VMEM((4, 16, 16, HH), BF16),
            pltpu.VMEM((4, 16, HH), F32),
            pltpu.VMEM((LAST, 16, 512), BF16),
            pltpu.VMEM((LAST, 16, 512), BF16),
            pltpu.VMEM((16, 512), F32),
            pltpu.VMEM((16, 8, HH), F32),
            pltpu.VMEM((128, 128), F32),
            pltpu.VMEM((128, 128), F32),
            pltpu.VMEM((2, 8, 128), F32),
            pltpu.VMEM((16, 8, 128), F32),
            pltpu.VMEM((8, 8, 128), F32),
            pltpu.VMEM((2, 8, 128), F32),
            pltpu.VMEM((TH, 128), F32),
            pltpu.VMEM((8, 8, 128), F32),
            pltpu.VMEM((2, 8, 128), F32),
            pltpu.VMEM((16, 8, 128), F32),
            pltpu.VMEM((2, 8, 128), F32),
            pltpu.VMEM((1, ROWS), jnp.int32),
            pltpu.VMEM((1, ROWS), jnp.int32),
            dma((5,)),
            dma((4,)), dma((4,)),
            dma((3,)), dma((3,)),
            dma((2,)), dma((2,)),
            dma((2,)), dma((2,)),
            dma((2,)), dma((6,)),
            dma((4,)), dma((4,)),
            dma((2,)), dma((2,)),
            dma, dma,
            dma((4,)), dma((4,)),
        ],
        compiler_params=pltpu.CompilerParams(
            collective_id=0, has_side_effects=True, vmem_limit_bytes=VMEM_BYTES
        ),
        cost_estimate=pl.CostEstimate(
            flops=2 * ROWS * COLS * HS, bytes_accessed=6 * 1024 * 1024, transcendentals=3 * ROWS * COLS
        ),
        name="distill",
    )(
        logits.reshape(ROWS, 2 * COLS),
        segment_ids.reshape(1, ROWS),
        token_mask.reshape(1, ROWS),
        student_head.reshape(BLK, HS),
    )
    return grad, hidden, loss.reshape(())


def solution(mesh):
    placed = (P("grp", "tok", "vocab"), P("tok"), P("tok"), P(("vocab", "grp"), "tok", None, None))
    return jax.shard_map(
        per_device,
        mesh=mesh,
        in_specs=placed,
        out_specs=(P("tok", ("vocab", "grp")), P("tok", "grp"), P()),
        check_vma=False,
    )
```

time: 141 us -> 115 us (0.82)
  Pallas kernels: 132 us -> 110 us
  local copies, waits for them, and re-layouts: 5.81 us -> 3.11 us
    pallas_call x1, Pallas kernels: 132 us -> 110 us  [per_device(): pl.pallas_call(kernel, out_shape=(jax.ShapeDtypeStruct((ROWS, COLS), BF16...]
    unnamed x10 -> x4, local copies, waits for them, and re-layouts: 5.81 us -> 3.11 us
where the time goes in v2:
time: 115 us
  Pallas kernels  110 us (96%)
  local copies, waits for them, and re-layouts  3.11 us (3%)
  between operations  2.34 us (2%)
    pallas_call x1, Pallas kernels, per_device(): pl.pallas_call(kernel, out_shape=(jax.ShapeDtypeStruct((ROWS, COLS), BF16...  110 us
    unnamed x4, local copies, waits for them, and re-layouts  3.11 us

profile of v2, /device:TPU:1, one launch (start us, length us, event | category | flops | bytes accessed | tf_op | source)
XLA Modules:
  0.0 115.2 jit_solution(11974548364496711700)
XLA Ops:
  0.6 109.8 %distill.1 = (bf16[128,4096]{1,0:T(8,128)(2,1)}, f32[128,896]{1,0:T(8,128)}, f32[1,1]{1,0:T(1,128)}) custom-call(bf16[128,8192]{1,0:T(8,128)(2,1)} %bitcast.5, s32[1,128]{1,0:T(1,128)} %bitcast.7, s32[1,128]{1,0:T(1,128)} %bitcast.8, bf16[256,1792]{1,0:T(8,128)(2,1)} %bitcast.6), custom_call_target="tpu_custom_call" | custom-call | flops 1879048192 | bytes 6291456 | tf_op jit(solution)/shard_map/distill/pallas_call | solution.py:368
  110.4 0.0 copy-start
  110.4 2.3 %copy.10 = bf16[128,4096]{1,0:T(8,128)(2,1)} copy(bf16[128,4096]{1,0:T(8,128)(2,1)} %get-tuple-element.12) | data formatting | bytes 2097152
  112.8 0.0 copy-done
  112.8 0.8 copy.11
Async XLA Ops:
  110.4 2.4 %copy-start = (f32[128,896]{1,0:T(8,128)S(1)}, f32[128,896]{1,0:T(8,128)}, u32[]{:S(2)}) copy-start(f32[128,896]{1,0:T(8,128)} %get-tuple-element.13) | copy-start | bytes 1376260

commit v3 on v2

--- a/solution.py
+++ b/solution.py
@@ -22,8 +22,16 @@
 LAST = 7
 
 
+def rem(a, b):
+    return lax.rem(jnp.int32(a), jnp.int32(b))
+
+
+def div(a, b):
+    return lax.div(jnp.int32(a), jnp.int32(b))
+
+
 def off(p):
-    return (4 + ((p + 1) // 2) * (1 - 2 * (p % 2))) % 8
+    return rem(4 + div(p + 1, 2) * (1 - 2 * rem(p, 2)), 8)
 
 
 def kernel(
@@ -37,22 +45,22 @@
     z = lax.axis_index("tok")
     v = lax.axis_index("vocab")
     g = lax.axis_index("grp")
-    c = v % 2
-    xl = (v // 2) % 2
-    y = v // 4
-    j = v // 2
-    par = z % 2
+    c = rem(v, 2)
+    xl = rem(div(v, 2), 2)
+    y = div(v, 4)
+    j = div(v, 2)
+    par = rem(z, 2)
     oc = 1 - c
     og = 1 - g
     ov = v + 1 - 2 * c
-    mate = (z + 1 + 14 * ((z + c) % 2)) % NT
-    my_pos = (z + c) % 2
+    mate = rem(z + 1 + 14 * rem(z + c, 2), NT)
+    my_pos = rem(z + c, 2)
 
     def plane(r):
-        h, a, b = r // 8, (r // 2) % 4, r % 2
-        y2 = (y + 4 - a) % 4
-        x2 = (xl + 2 - b) % 2
-        g2 = (g + 2 - h) % 2
+        h, a, b = div(r, 8), rem(div(r, 2), 4), rem(r, 2)
+        y2 = rem(y + 4 - a, 4)
+        x2 = rem(xl + 2 - b, 2)
+        g2 = rem(g + 2 - h, 2)
         return y2 * 2 + x2, g2
 
     def plane_dev(r, core):
@@ -60,7 +68,7 @@
         return (z, j2 * 2 + core, g2)
 
     def column(p):
-        return (z + NT - 2 * off(p)) % NT
+        return rem(z + NT - 2 * off(p), NT)
 
     def send(src, dst, ss, rs, dev):
         copy = pltpu.make_async_remote_copy(
@@ -122,12 +130,11 @@
     other_cols = pl.ds(pl.multiple_of(COLS * og, COLS), COLS)
 
     def exchange(t):
-        rows = pl.ds(TH * t, TH)
+        rows = pl.ds(pl.multiple_of(TH * t, TH), TH)
         send(lg_hbm.at[rows, other_cols], ao.at[rows], x_s.at[t], x_r.at[t], (z, v, og))
 
     send(st.at[0], st.at[1], t_s.at[0], t_r.at[0], core_mate)
     exchange(0)
-    exchange(1)
 
     in_seg.wait()
     in_mask.wait()
@@ -148,7 +155,7 @@
     sub = lax.broadcasted_iota(jnp.int32, (8, ROWS), 0)
     sb[0] = jnp.where(sub == 0, top, mass)
     loop(1, 16, lambda r: send(sb.at[0], sb.at[r], t_s.at[1], t_r.at[1], plane_dev(r, c)))
-    exchange(2)
+    exchange(1)
 
     wait(cz.at[pl.ds(0, LAST)], c_r.at[0])
     part = cz[0]
@@ -156,7 +163,6 @@
         part = part + cz[p]
     cm[0] = part
     send(cm.at[0], cm.at[1], c_s.at[1], c_r.at[1], (mate, v, g))
-    exchange(3)
 
     wait(cm.at[1], c_r.at[1])
     sizes = jnp.sum(cm[0] + cm[1], axis=1, keepdims=True)
@@ -183,13 +189,13 @@
     sign = jnp.where(g == 0, -1.0, 1.0).astype(F32)
 
     def block(t, p):
-        i = (z // 2 + 8 - off(p)) % 8
-        first = (2 * i + c * (15 + 2 * par)) % 16
+        i = rem(div(z, 2) + 8 - off(p), 8)
+        first = rem(2 * i + c * (15 + 2 * par), 16)
         rows = pl.ds(pl.multiple_of(TH * t, TH), TH)
         stats = col[rows, :]
         own_l, other_l, wgt = stats[:, 0:1], stats[:, 1:2], stats[:, 2:3]
         scale = (SOFTEN * sign) * wgt
-        for n, k in enumerate((first, (first + 1) % 16)):
+        for n, k in enumerate((first, rem(first + 1, 16))):
             cols = pl.ds(pl.multiple_of(BLK * k, BLK), BLK)
             own_at = pl.ds(pl.multiple_of(COLS * g + BLK * k, BLK), BLK)
             log_own = lg[rows, own_at].astype(F32) * (1.0 / SOFTEN) - own_l
@@ -204,23 +210,27 @@
 
     def chunk(t):
         wait(ao.at[pl.ds(pl.multiple_of(TH * t, TH), TH)], x_r.at[t])
+        pl.when(t < 2)(lambda: exchange(t + 2))
         there = pl.ds(pl.multiple_of(16 * t, 16), 16)
 
         def place(p):
             block(t, p)
-            for e in range(2):
-                here = pl.ds(pl.multiple_of(TH * t + 16 * e, 16), 16)
-                send(
-                    gb.at[p, here], grx.at[c, p, there], g_s.at[0], g_r.at[2 * (t // 2) + p // 4],
-                    (column(p), 2 * j + e, g),
-                )
+            pl.when(t < 2)(lambda: ship_block(t, p))
 
         loop(0, LAST, place)
         block(t, LAST)
         mine = pl.ds(pl.multiple_of(TH * t + 16 * c, 16), 16)
         theirs = pl.ds(pl.multiple_of(TH * t + 16 * oc, 16), 16)
         grx[c, LAST, there, :] = gb[LAST, mine, :]
-        send(gb.at[LAST, theirs], grx.at[c, LAST, there], g_s.at[1], g_r.at[4 + t // 2], core_mate)
+        send(gb.at[LAST, theirs], grx.at[c, LAST, there], g_s.at[4 + t], g_r.at[4 + t], core_mate)
+
+    def ship_block(t, p):
+        there = pl.ds(pl.multiple_of(16 * t, 16), 16)
+        for e in range(2):
+            here = pl.ds(pl.multiple_of(TH * t + 16 * e, 16), 16)
+            send(
+                gb.at[p, here], grx.at[c, p, there], g_s.at[t], g_r.at[t], (column(p), 2 * j + e, g)
+            )
 
     loop(0, 4, chunk)
 
@@ -235,11 +245,11 @@
 
     out_row = lax.broadcasted_iota(jnp.int32, (128, 128), 0)
     in_row = lax.broadcasted_iota(jnp.int32, (128, 128), 1)
-    source = ((out_row // 4) % 4) * TH + (out_row // 16) * 4 + out_row % 4
+    source = ((out_row // 2) % 8) * 16 + (out_row // 16) * 2 + out_row % 2
     order = (in_row == source).astype(F32).astype(BF16)
 
-    wait(hb.at[oc, (z + oc) % 2], h_r.at[1])
-    wait(hb.at[oc, 1 - (z + oc) % 2], h_r.at[2])
+    wait(hb.at[oc, rem(z + oc, 2)], h_r.at[1])
+    wait(hb.at[oc, 1 - rem(z + oc, 2)], h_r.at[2])
 
     def loss_plane():
         wait(lp.at[pl.ds(1, 15)], l_r.at[2])
@@ -257,35 +267,30 @@
         rsum[q] = total
 
     def multiply(q):
-        th, bh = q // 2, q % 2
-        rows = pl.ds(pl.multiple_of(TH * th, TH), TH)
-
-        @pl.when(bh == 0)
+        rows = pl.ds(pl.multiple_of(16 * q, 16), 16)
+
+        @pl.when(q < 2)
         def _():
-            wait(grx.at[:, pl.ds(0, 4), rows], g_r.at[2 * th])
-
-        @pl.when(bh == 1)
-        def _():
-            wait(grx.at[:, pl.ds(4, 3), rows], g_r.at[2 * th + 1])
-            wait(grx.at[oc, LAST, rows], g_r.at[4 + th])
-
+            wait(grx.at[:, pl.ds(0, LAST), rows], g_s.at[q])
+            loop(0, LAST, lambda p: ship_block(q + 2, p))
+
+        wait(grx.at[:, pl.ds(0, LAST), rows], g_r.at[q])
+        wait(grx.at[oc, LAST, rows], g_r.at[4 + q])
         xs = []
         for b in range(2):
-            x = grx[b, pl.ds(4 * bh, 4), rows, :].reshape(128, 2 * BLK)
+            x = grx[b, :, rows, :].reshape(128, 2 * BLK)
             xs.append(jnp.dot(order, x, preferred_element_type=F32).astype(BF16))
-        for gg in range(2):
-            part = jnp.dot(
-                xs[0], hb[0, :, :, HH * gg:HH * gg + HH].reshape(512, HH), preferred_element_type=F32
-            ) + jnp.dot(
-                xs[1], hb[1, :, :, HH * gg:HH * gg + HH].reshape(512, HH), preferred_element_type=F32
-            )
-            pb[q, gg] = part.astype(BF16).reshape(8, 16, HH)
-
         def share(r):
             j2, g2 = plane(r)
             send(pb.at[q, g2, j2], rb.at[q, r], p_s.at[q], p_r.at[q], (z, j2 * 2 + c, g2))
 
-        loop(1, 16, share)
+        for gg, first, last in ((og, 8, 16), (g, 1, 8)):
+            cols = pl.ds(pl.multiple_of(HH * gg, 128), HH)
+            part = jnp.dot(
+                xs[0], hb[0, :, :, cols].reshape(512, HH), preferred_element_type=F32
+            ) + jnp.dot(xs[1], hb[1, :, :, cols].reshape(512, HH), preferred_element_type=F32)
+            pb[q, gg] = part.astype(BF16).reshape(8, 16, HH)
+            loop(first, last, share)
 
         @pl.when(q > 0)
         def _():
@@ -293,32 +298,46 @@
 
         pl.when(q == 1)(loss_plane)
 
-    def spread(bh):
-        for bb in range(4):
-            p = 4 * bh + bb
-            x = jnp.concatenate([rsum[bh, 4 * bb:4 * bb + 4], rsum[2 + bh, 4 * bb:4 * bb + 4]], axis=0)
-            x = jnp.concatenate([x[:, :512], jnp.pad(x[:, 512:], ((0, 0), (0, 128)))], axis=0)
+        @pl.when(q == 3)
+        def _():
+            for done in range(3):
+                pack(done)
+            spread(0, 3, 0)
+
+    def pack(q):
+        for p in range(8):
+            pair = rsum[q, 2 * p:2 * p + 2]
+            x = jnp.concatenate(
+                [pair[:, 128 * k:128 * k + 128] for k in range(7)] + [jnp.zeros((2, 128), F32)], axis=0
+            )
             if p == LAST:
-                own[...] = x
+                own[:, 128 * q:128 * q + 128] = x
             else:
-                zs[p] = x.astype(BF16)
-                send(zs.at[p], zr.at[p], z_s.at[bh], z_r.at[bh], ((z + 2 * off(p)) % NT, v, g))
+                zs[p, :, 128 * q:128 * q + 128] = x.astype(BF16)
+
+    def spread(first, last, k):
+        cols = slice(128 * first, 128 * last)
+        for p in range(LAST):
+            send(
+                zs.at[p, :, cols], zr.at[p, :, cols], z_s.at[k], z_r.at[k],
+                (rem(z + 2 * off(p), NT), v, g),
+            )
 
     loop(0, 4, multiply)
-    spread(0)
     wait(lc.at[1], l_r.at[3])
     lz[LAST] = lc[0] + lc[1]
     loop(0, LAST, lambda p: send(lz.at[LAST], lz.at[p], l_s.at[0], l_r.at[0], (column(p), v, g)))
     reduce(3)
-    spread(1)
-
-    wait(zr.at[pl.ds(0, 4)], z_r.at[0])
-    wait(zr.at[pl.ds(4, 3)], z_r.at[1])
+    pack(3)
+    spread(3, 4, 1)
+
+    wait(zr.at[:, :, 0:384], z_r.at[0])
+    wait(zr.at[:, :, 384:512], z_r.at[1])
     total = own[...]
     for p in range(LAST):
         total = total + zr[p].astype(F32)
     slot = 8 * c + j
-    fb[slot] = jnp.concatenate([total[:8], total[8:, :384]], axis=1)
+    fb[slot] = total
     loop(1, 8, lambda r: send(fb.at[slot], fb.at[slot], f_s, f_r, plane_dev(r, c)))
     loop(0, 8, lambda r: send(fb.at[slot], fb.at[slot], f_s, f_r, plane_dev(r, oc)))
 
@@ -330,8 +349,11 @@
     send(lm.at[0], lm.at[1], l_s.at[1], l_r.at[1], (mate, v, g))
 
     loop(0, 4, lambda t: wait(ao.at[pl.ds(0, TH)], x_s.at[t]))
-    wait(grx.at[:, pl.ds(0, LAST)], g_s.at[0])
-    wait(grx.at[0, LAST], g_s.at[1])
+    for t in range(4):
+        rows = pl.ds(16 * t, 16)
+        if t >= 2:
+            wait(grx.at[:, pl.ds(0, LAST), rows], g_s.at[t])
+        wait(grx.at[0, LAST, rows], g_s.at[4 + t])
     loop(0, 3, lambda k: wait(hb.at[0, 0], h_s.at[k]))
     wait(cz.at[pl.ds(0, LAST)], c_s.at[0])
     wait(cm.at[1], c_s.at[1])
@@ -339,8 +361,8 @@
     wait(sb.at[pl.ds(1, 15)], t_s.at[1])
     out_own.wait()
     loop(0, 4, lambda q: wait(rb.at[q, pl.ds(1, 15)], p_s.at[q]))
-    wait(zr.at[pl.ds(0, 4)], z_s.at[0])
-    wait(zr.at[pl.ds(4, 3)], z_s.at[1])
+    wait(zr.at[:, :, 0:384], z_s.at[0])
+    wait(zr.at[:, :, 384:512], z_s.at[1])
     wait(lz.at[pl.ds(0, LAST)], l_s.at[0])
     wait(lm.at[1], l_s.at[1])
     wait(lp.at[pl.ds(1, 15)], l_s.at[2])
@@ -352,12 +374,12 @@
     for t in range(4):
         for e in range(2):
             for h in range(2):
-                n = 8 * e + 4 * (t % 2) + 2 * h
-                at = 4 * (t // 2)
+                n = 8 * e + 4 * h
                 row = TH * t + 16 * e + 8 * h
-                hid_out[row:row + 8, :] = jnp.concatenate(
-                    [fb[n, at:at + 4], fb[n + 1, at:at + 4]], axis=0
-                )
+                for k in range(7):
+                    hid_out[row:row + 8, 128 * k:128 * k + 128] = jnp.concatenate(
+                        [fb[n + i, 2 * k:2 * k + 2, 128 * t:128 * t + 128] for i in range(4)], axis=0
+                    )
     wait(fb.at[pl.ds(0, 15)], f_s)
 
 
@@ -387,7 +409,7 @@
             pltpu.VMEM((LAST, 16, 512), BF16),
             pltpu.VMEM((LAST, 16, 512), BF16),
             pltpu.VMEM((16, 512), F32),
-            pltpu.VMEM((16, 8, HH), F32),
+            pltpu.VMEM((16, 16, 512), F32),
             pltpu.VMEM((128, 128), F32),
             pltpu.VMEM((128, 128), F32),
             pltpu.VMEM((2, 8, 128), F32),
@@ -406,7 +428,7 @@
             dma((3,)), dma((3,)),
             dma((2,)), dma((2,)),
             dma((2,)), dma((2,)),
-            dma((2,)), dma((6,)),
+            dma((8,)), dma((8,)),
             dma((4,)), dma((4,)),
             dma((2,)), dma((2,)),
             dma, dma,

time: 115 us -> 109 us (0.948)
  Pallas kernels: 110 us -> 104 us
    pallas_call x1, Pallas kernels: 110 us -> 104 us  [per_device(): pl.pallas_call(kernel, out_shape=(jax.ShapeDtypeStruct((ROWS, COLS), BF16...]
where the time goes in v3:
time: 109 us
  Pallas kernels  104 us (95%)
  local copies, waits for them, and re-layouts  3.11 us (3%)
  between operations  2.34 us (2%)
    pallas_call x1, Pallas kernels, per_device(): pl.pallas_call(kernel, out_shape=(jax.ShapeDtypeStruct((ROWS, COLS), BF16...  104 us
    unnamed x4, local copies, waits for them, and re-layouts  3.11 us

profile of v3, /device:TPU:1, one launch (start us, length us, event | category | flops | bytes accessed | tf_op | source)
XLA Modules:
  0.0 109.2 jit_solution(1079804871031572331)
XLA Ops:
  0.6 103.8 %distill.1 = (bf16[128,4096]{1,0:T(8,128)(2,1)}, f32[128,896]{1,0:T(8,128)}, f32[1,1]{1,0:T(1,128)}) custom-call(bf16[128,8192]{1,0:T(8,128)(2,1)} %bitcast.5, s32[1,128]{1,0:T(1,128)} %bitcast.7, s32[1,128]{1,0:T(1,128)} %bitcast.8, bf16[256,1792]{1,0:T(8,128)(2,1)} %bitcast.6), custom_call_target="tpu_custom_call" | custom-call | flops 1879048192 | bytes 6291456 | tf_op jit(solution)/shard_map/distill/pallas_call | solution.py:390
  104.4 0.0 copy-start
  104.4 2.3 %copy.10 = bf16[128,4096]{1,0:T(8,128)(2,1)} copy(bf16[128,4096]{1,0:T(8,128)(2,1)} %get-tuple-element.12) | data formatting | bytes 2097152
  106.8 0.0 copy-done
  106.8 0.8 copy.11
Async XLA Ops:
  104.4 2.4 %copy-start = (f32[128,896]{1,0:T(8,128)S(1)}, f32[128,896]{1,0:T(8,128)}, u32[]{:S(2)}) copy-start(f32[128,896]{1,0:T(8,128)} %get-tuple-element.13) | copy-start | bytes 1376260

commit v4 on v3

--- a/solution.py
+++ b/solution.py
@@ -269,6 +269,12 @@
     def multiply(q):
         rows = pl.ds(pl.multiple_of(16 * q, 16), 16)
 
+        @pl.when(q == 3)
+        def _():
+            reduce(2)
+            for done in range(3):
+                pack(done)
+
         @pl.when(q < 2)
         def _():
             wait(grx.at[:, pl.ds(0, LAST), rows], g_s.at[q])
@@ -292,17 +298,12 @@
             pb[q, gg] = part.astype(BF16).reshape(8, 16, HH)
             loop(first, last, share)
 
-        @pl.when(q > 0)
+        @pl.when((q == 1) | (q == 2))
         def _():
             reduce(q - 1)
 
         pl.when(q == 1)(loss_plane)
-
-        @pl.when(q == 3)
-        def _():
-            for done in range(3):
-                pack(done)
-            spread(0, 3, 0)
+        pl.when(q == 3)(lambda: spread(0, 3, 0))
 
     def pack(q):
         for p in range(8):
@@ -331,15 +332,21 @@
     pack(3)
     spread(3, 4, 1)
 
-    wait(zr.at[:, :, 0:384], z_r.at[0])
-    wait(zr.at[:, :, 384:512], z_r.at[1])
-    total = own[...]
-    for p in range(LAST):
-        total = total + zr[p].astype(F32)
     slot = 8 * c + j
-    fb[slot] = total
-    loop(1, 8, lambda r: send(fb.at[slot], fb.at[slot], f_s, f_r, plane_dev(r, c)))
-    loop(0, 8, lambda r: send(fb.at[slot], fb.at[slot], f_s, f_r, plane_dev(r, oc)))
+
+    def gather(first, last, k):
+        cols = slice(128 * first, 128 * last)
+        wait(zr.at[:, :, cols], z_r.at[k])
+        total = own[:, cols]
+        for p in range(LAST):
+            total = total + zr[p, :, cols].astype(F32)
+        fb[slot, :, cols] = total
+        mine = fb.at[slot, :, cols]
+        loop(1, 8, lambda r: send(mine, mine, f_s.at[k], f_r.at[k], plane_dev(r, c)))
+        loop(0, 8, lambda r: send(mine, mine, f_s.at[k], f_r.at[k], plane_dev(r, oc)))
+
+    gather(0, 3, 0)
+    gather(3, 4, 1)
 
     wait(lz.at[pl.ds(0, LAST)], l_r.at[0])
     part = lz[0]
@@ -370,8 +377,7 @@
     wait(lm.at[1], l_r.at[1])
     loss_out[...] = jnp.sum(lm[0] + lm[1], keepdims=True) * (SOFTEN * SOFTEN) / (NT * ROWS)
 
-    wait(fb.at[pl.ds(0, 15)], f_r)
-    for t in range(4):
+    def assemble(t):
         for e in range(2):
             for h in range(2):
                 n = 8 * e + 4 * h
@@ -380,7 +386,14 @@
                     hid_out[row:row + 8, 128 * k:128 * k + 128] = jnp.concatenate(
                         [fb[n + i, 2 * k:2 * k + 2, 128 * t:128 * t + 128] for i in range(4)], axis=0
                     )
-    wait(fb.at[pl.ds(0, 15)], f_s)
+
+    wait(fb.at[pl.ds(0, 15), :, 0:384], f_r.at[0])
+    for t in range(3):
+        assemble(t)
+    wait(fb.at[pl.ds(0, 15), :, 0:384], f_s.at[0])
+    wait(fb.at[pl.ds(0, 15), :, 384:512], f_r.at[1])
+    assemble(3)
+    wait(fb.at[pl.ds(0, 15), :, 384:512], f_s.at[1])
 
 
 def per_device(logits, segment_ids, token_mask, student_head):
@@ -431,7 +444,7 @@
             dma((8,)), dma((8,)),
             dma((4,)), dma((4,)),
             dma((2,)), dma((2,)),
-            dma, dma,
+            dma((2,)), dma((2,)),
             dma((4,)), dma((4,)),
         ],
         compiler_params=pltpu.CompilerParams(

time: 109 us -> 108 us (level)
  no operation moved by 1% of the time
where the time goes in v4:
time: 108 us
  Pallas kernels  103 us (95%)
  local copies, waits for them, and re-layouts  3.11 us (3%)
  between operations  2.34 us (2%)
    pallas_call x1, Pallas kernels, per_device(): pl.pallas_call(kernel, out_shape=(jax.ShapeDtypeStruct((ROWS, COLS), BF16...  103 us
    unnamed x4, local copies, waits for them, and re-layouts  3.11 us

profile of v4, /device:TPU:1, one launch (start us, length us, event | category | flops | bytes accessed | tf_op | source)
XLA Modules:
  0.0 108.3 jit_solution(16945418572186901822)
XLA Ops:
  0.6 102.8 %distill.1 = (bf16[128,4096]{1,0:T(8,128)(2,1)}, f32[128,896]{1,0:T(8,128)}, f32[1,1]{1,0:T(1,128)}) custom-call(bf16[128,8192]{1,0:T(8,128)(2,1)} %bitcast.5, s32[1,128]{1,0:T(1,128)} %bitcast.7, s32[1,128]{1,0:T(1,128)} %bitcast.8, bf16[256,1792]{1,0:T(8,128)(2,1)} %bitcast.6), custom_call_target="tpu_custom_call" | custom-call | flops 1879048192 | bytes 6291456 | tf_op jit(solution)/shard_map/distill/pallas_call | solution.py:403
  103.5 0.0 copy-start
  103.5 2.3 %copy.10 = bf16[128,4096]{1,0:T(8,128)(2,1)} copy(bf16[128,4096]{1,0:T(8,128)(2,1)} %get-tuple-element.12) | data formatting | bytes 2097152
  105.8 0.0 copy-done
  105.8 0.8 copy.11
Async XLA Ops:
  103.5 2.4 %copy-start = (f32[128,896]{1,0:T(8,128)S(1)}, f32[128,896]{1,0:T(8,128)}, u32[]{:S(2)}) copy-start(f32[128,896]{1,0:T(8,128)} %get-tuple-element.13) | copy-start | bytes 1376260

commit v5 on v4

--- a/solution.py
+++ b/solution.py
@@ -215,7 +215,7 @@
 
         def place(p):
             block(t, p)
-            pl.when(t < 2)(lambda: ship_block(t, p))
+            pl.when(t < 3)(lambda: ship_block(t, p))
 
         loop(0, LAST, place)
         block(t, LAST)
@@ -275,10 +275,10 @@
             for done in range(3):
                 pack(done)
 
-        @pl.when(q < 2)
+        @pl.when(q == 0)
         def _():
             wait(grx.at[:, pl.ds(0, LAST), rows], g_s.at[q])
-            loop(0, LAST, lambda p: ship_block(q + 2, p))
+            loop(0, LAST, lambda p: ship_block(q + 3, p))
 
         wait(grx.at[:, pl.ds(0, LAST), rows], g_r.at[q])
         wait(grx.at[oc, LAST, rows], g_r.at[4 + q])
@@ -358,7 +358,7 @@
     loop(0, 4, lambda t: wait(ao.at[pl.ds(0, TH)], x_s.at[t]))
     for t in range(4):
         rows = pl.ds(16 * t, 16)
-        if t >= 2:
+        if t >= 1:
             wait(grx.at[:, pl.ds(0, LAST), rows], g_s.at[t])
         wait(grx.at[0, LAST, rows], g_s.at[4 + t])
     loop(0, 3, lambda k: wait(hb.at[0, 0], h_s.at[k]))

time: 108 us -> 108 us (level)
  no operation moved by 1% of the time
where the time goes in v5:
time: 108 us
  Pallas kernels  102 us (94%)
  local copies, waits for them, and re-layouts  3.11 us (3%)
  between operations  2.34 us (2%)
    pallas_call x1, Pallas kernels, per_device(): pl.pallas_call(kernel, out_shape=(jax.ShapeDtypeStruct((ROWS, COLS), BF16...  102 us
    unnamed x4, local copies, waits for them, and re-layouts  3.11 us

profile of v5, /device:TPU:1, one launch (start us, length us, event | category | flops | bytes accessed | tf_op | source)
XLA Modules:
  0.0 107.8 jit_solution(8443878424226424637)
XLA Ops:
  0.6 102.3 %distill.1 = (bf16[128,4096]{1,0:T(8,128)(2,1)}, f32[128,896]{1,0:T(8,128)}, f32[1,1]{1,0:T(1,128)}) custom-call(bf16[128,8192]{1,0:T(8,128)(2,1)} %bitcast.5, s32[1,128]{1,0:T(1,128)} %bitcast.7, s32[1,128]{1,0:T(1,128)} %bitcast.8, bf16[256,1792]{1,0:T(8,128)(2,1)} %bitcast.6), custom_call_target="tpu_custom_call" | custom-call | flops 1879048192 | bytes 6291456 | tf_op jit(solution)/shard_map/distill/pallas_call | solution.py:403
  103.0 0.0 copy-start
  103.0 2.3 %copy.10 = bf16[128,4096]{1,0:T(8,128)(2,1)} copy(bf16[128,4096]{1,0:T(8,128)(2,1)} %get-tuple-element.12) | data formatting | bytes 2097152
  105.3 0.0 copy-done
  105.3 0.8 copy.11
Async XLA Ops:
  103.0 2.4 %copy-start = (f32[128,896]{1,0:T(8,128)S(1)}, f32[128,896]{1,0:T(8,128)}, u32[]{:S(2)}) copy-start(f32[128,896]{1,0:T(8,128)} %get-tuple-element.13) | copy-start | bytes 1376260
